TPU v7x, 128 devices: a whole 4x4x4 slice. The times are simulated.
128 devices in a mesh: dp: 4 (over x), ctx: 32 (over z, y, core).
Axes of the slice: x: 4, y: 4, z: 4, core: 2. Of those that a mesh axis runs over, the one named last changes fastest.
Arguments:
- inputs: bfloat16 [16384, 896], P(('dp', 'ctx')), may hold values from -6 to 6
- cotangent: bfloat16 [16384, 896], P(('dp', 'ctx')), may hold values from -6 to 6
- span_order: int32 [64], replicated, may hold values from 0 to 63, as said below
- positions: int32 [16384], P(('dp', 'ctx')), may hold values from 0 to 1023, as said below
- attn_gain: bfloat16 [896], P('dp'), may hold values from 0.5 to 1.5
- qkv_weight: bfloat16 [896, 1152], P('dp'), may hold values from -0.1875 to 0.1875
- qkv_bias: bfloat16 [1152], P('dp'), may hold values from -3 to 3
- out_weight: bfloat16 [896, 896], P('dp'), may hold values from -0.375 to 0.375
- mlp_gain: bfloat16 [896], P('dp'), may hold values from 0.5 to 1.5
- gate_weight: bfloat16 [896, 4864], P('dp'), may hold values from -0.1875 to 0.1875
- up_weight: bfloat16 [896, 4864], P('dp'), may hold values from -0.1875 to 0.1875
- down_weight: bfloat16 [4864, 896], P('dp'), may hold values from -0.078125 to 0.078125
Outputs:
- output: bfloat16 [16384, 896], P(('dp', 'ctx'))
- input_grad: bfloat16 [16384, 896], P(('dp', 'ctx'))
- attn_gain_grad: float32 [896], P('dp')
- qkv_weight_grad: float32 [896, 1152], P('dp')
- qkv_bias_grad: float32 [1024], P('dp')
- value_bias_grad: float32 [128], P('dp')
- out_weight_grad: float32 [896, 896], P('dp')
- mlp_gain_grad: float32 [896], P('dp')
- gate_weight_grad: float32 [896, 4864], P('dp')
- up_weight_grad: float32 [896, 4864], P('dp')
- down_weight_grad: float32 [4864, 896], P('dp')
Inputs may be any that keep to these rules, and one draw needn't show every extreme that they name: `span_order`: entries 2c and 2c + 1 hold two spans j and 63 - j, in either order; every span appears once. `positions`: each token's position within its document. Documents are runs of consecutive places of a sequence, none longer than 1024 tokens, and positions count from 0 at a run's start, increasing by one along place.
All inputs are finite; a program needn't handle non-finite values.
Results may differ from a plain program's by a relative error of at most 0.03.
Values may be sent and summed in bfloat16 or wider, within the bound.
A program may use at most 192 MiB of HBM per device.

v0:
```python
import jax
import jax.numpy as jnp
from jax import lax
from jax.sharding import PartitionSpec as P

QH = 14
KVH = 2
HD = 64


norm_eps = 1e-06
rope_base = 1000000.0
masked_score = -1e30


def rms_apply(values, gain):
    mean_square = jnp.mean(values * values, axis=-1, keepdims=True)
    return values * lax.rsqrt(mean_square + norm_eps) * gain


def half_turn(values):
    middle = values.shape[-1] // 2
    return jnp.concatenate([-values[..., middle:], values[..., :middle]], axis=-1)


def rotate(values, cosine, sine):
    return values * cosine + half_turn(values) * sine


def rope_tables(positions, head_dim):
    middle = head_dim // 2
    inverse = rope_base ** (-(jnp.arange(middle).astype(jnp.float32) * 2.0) / head_dim)
    angles = positions.astype(jnp.float32)[:, None] * inverse[None, :]
    angles = jnp.concatenate([angles, angles], axis=-1)
    return (jnp.cos(angles), jnp.sin(angles))


def span_lookup(table, slots):
    picked = slots[:, None] == jnp.arange(table.shape[0], dtype=jnp.int32)[None, :]
    return jnp.sum(jnp.where(picked, table[None, :], 0), axis=1)


def swiglu(gate_in, up_in):
    return jax.nn.silu(gate_in) * up_in


def body(
    inputs,
    cotangent,
    span_order,
    positions,
    attn_gain,
    qkv_weight,
    qkv_bias,
    out_weight,
    mlp_gain,
    gate_weight,
    up_weight,
    down_weight,
):
    token_count = inputs.shape[0]
    span_rows = token_count // 2
    head_dim = HD
    query_heads = QH
    kv_heads = KVH
    group_size = query_heads // kv_heads
    score_scale = head_dim ** (-0.5)
    q_cols = query_heads * head_dim
    k_cols = kv_heads * head_dim
    seq_length = token_count * lax.axis_size("ctx")
    key_block = min(1024, seq_length)
    block_count = seq_length // key_block
    device_slot = lax.axis_index("ctx")
    local_slots = jnp.arange(token_count, dtype=jnp.int32)
    query_places = (
        span_lookup(span_order, 2 * device_slot + local_slots // span_rows) * span_rows
        + local_slots % span_rows
    )
    all_slots = jnp.arange(seq_length, dtype=jnp.int32)
    key_places = span_lookup(span_order, all_slots // span_rows) * span_rows + all_slots % span_rows
    key_places = key_places.reshape(block_count, key_block)
    gain_one, qkv_full, bias_full, out_full = (
        lax.all_gather(attn_gain, "dp", axis=0, tiled=True),
        lax.all_gather(qkv_weight, "dp", axis=0, tiled=True),
        lax.all_gather(qkv_bias, "dp", axis=0, tiled=True),
        lax.all_gather(out_weight, "dp", axis=0, tiled=True),
    )
    inputs_wide = inputs.astype(jnp.float32)
    gain_one_wide = gain_one.astype(jnp.float32)
    normed_one = rms_apply(inputs_wide, gain_one_wide).astype(jnp.bfloat16)
    mixed_proj = jnp.dot(
        normed_one, qkv_full, preferred_element_type=jnp.float32
    ) + bias_full.astype(jnp.float32)
    cosine, sine = rope_tables(positions, head_dim)
    cosine = cosine[:, None, :]
    sine = sine[:, None, :]
    query_rot = rotate(
        mixed_proj[:, :q_cols].reshape(token_count, query_heads, head_dim), cosine, sine
    ).astype(jnp.bfloat16)
    key_rot = rotate(
        mixed_proj[:, q_cols : q_cols + k_cols].reshape(token_count, kv_heads, head_dim),
        cosine,
        sine,
    )
    key_rot = key_rot.astype(jnp.bfloat16).reshape(token_count, k_cols)
    value_low = mixed_proj[:, q_cols + k_cols :].astype(jnp.bfloat16)
    key_all, value_all = (
        lax.all_gather(key_rot, "ctx", axis=0, tiled=True),
        lax.all_gather(value_low, "ctx", axis=0, tiled=True),
    )
    key_blocks = key_all.reshape(block_count, key_block, kv_heads, head_dim)
    value_blocks = value_all.reshape(block_count, key_block, kv_heads, head_dim)
    query_grouped = query_rot.reshape(token_count, kv_heads, group_size, head_dim)

    def block_scores(key_part, place_part):
        scores = (
            jnp.einsum(
                "qhgd,khd->hgqk", query_grouped, key_part, preferred_element_type=jnp.float32
            )
            * score_scale
        )
        allowed = place_part[None, :] <= query_places[:, None]
        return jnp.where(allowed[None, None], scores, masked_score)

    def max_step(running, pieces):
        running_max, running_sum = running
        scores = block_scores(pieces[0], pieces[1])
        new_max = jnp.maximum(running_max, jnp.max(scores, axis=-1))
        new_sum = running_sum * jnp.exp(running_max - new_max) + jnp.sum(
            jnp.exp(scores - new_max[..., None]), axis=-1
        )
        return ((new_max, new_sum), None)

    start_max = jnp.full((kv_heads, group_size, token_count), masked_score, jnp.float32)
    start_sum = jnp.zeros((kv_heads, group_size, token_count), jnp.float32)
    (final_max, final_sum), unused = lax.scan(
        max_step, (start_max, start_sum), (key_blocks, key_places)
    )
    log_total = final_max + jnp.log(final_sum)

    def value_step(attended_sum, pieces):
        scores = block_scores(pieces[0], pieces[2])
        probs_low = jnp.exp(scores - log_total[..., None]).astype(jnp.bfloat16)
        return (
            attended_sum
            + jnp.einsum(
                "hgqk,khd->qhgd", probs_low, pieces[1], preferred_element_type=jnp.float32
            ),
            None,
        )

    start_total = jnp.zeros((token_count, kv_heads, group_size, head_dim), jnp.float32)
    attended_sum, unused = lax.scan(value_step, start_total, (key_blocks, value_blocks, key_places))
    attended_low = attended_sum.reshape(token_count, q_cols).astype(jnp.bfloat16)
    residual = inputs_wide + jnp.dot(attended_low, out_full, preferred_element_type=jnp.float32)
    gain_two, gate_full, up_full, down_full = (
        lax.all_gather(mlp_gain, "dp", axis=0, tiled=True),
        lax.all_gather(gate_weight, "dp", axis=0, tiled=True),
        lax.all_gather(up_weight, "dp", axis=0, tiled=True),
        lax.all_gather(down_weight, "dp", axis=0, tiled=True),
    )
    gain_two_wide = gain_two.astype(jnp.float32)
    normed_two = rms_apply(residual, gain_two_wide).astype(jnp.bfloat16)
    gate_proj = jnp.dot(normed_two, gate_full, preferred_element_type=jnp.float32)
    up_proj = jnp.dot(normed_two, up_full, preferred_element_type=jnp.float32)
    hidden_low = swiglu(gate_proj, up_proj).astype(jnp.bfloat16)
    output = (residual + jnp.dot(hidden_low, down_full, preferred_element_type=jnp.float32)).astype(
        jnp.bfloat16
    )
    d_hidden = jnp.dot(cotangent, down_full.T, preferred_element_type=jnp.float32)
    down_grad = jnp.dot(hidden_low.T, cotangent, preferred_element_type=jnp.float32)
    swiglu_back = jax.vjp(swiglu, gate_proj, up_proj)[1]
    d_gate, d_up = swiglu_back(d_hidden)
    d_gate = d_gate.astype(jnp.bfloat16)
    d_up = d_up.astype(jnp.bfloat16)
    gate_grad = jnp.dot(normed_two.T, d_gate, preferred_element_type=jnp.float32)
    up_grad = jnp.dot(normed_two.T, d_up, preferred_element_type=jnp.float32)
    d_normed_two = jnp.dot(d_gate, gate_full.T, preferred_element_type=jnp.float32) + jnp.dot(
        d_up, up_full.T, preferred_element_type=jnp.float32
    )
    norm_two_back = jax.vjp(rms_apply, residual, gain_two_wide)[1]
    d_resid_part, gain_two_grad = norm_two_back(d_normed_two)
    d_residual = d_resid_part + cotangent.astype(jnp.float32)
    d_branch = d_residual.astype(jnp.bfloat16)
    out_grad = jnp.dot(attended_low.T, d_branch, preferred_element_type=jnp.float32)
    d_attended = jnp.dot(d_branch, out_full.T, preferred_element_type=jnp.float32).astype(
        jnp.bfloat16
    )
    d_attended = d_attended.reshape(token_count, kv_heads, group_size, head_dim)
    row_delta = jnp.einsum("qhgd,qhgd->hgq", d_attended.astype(jnp.float32), attended_sum)

    def grad_step(d_query, pieces):
        key_part, value_part, place_part = pieces
        scores = block_scores(key_part, place_part)
        probs_full = jnp.exp(scores - log_total[..., None])
        probs_low = probs_full.astype(jnp.bfloat16)
        d_probs = jnp.einsum(
            "qhgd,khd->hgqk", d_attended, value_part, preferred_element_type=jnp.float32
        )
        d_scores = (probs_full * (d_probs - row_delta[..., None])).astype(jnp.bfloat16)
        d_query = (
            d_query
            + jnp.einsum("hgqk,khd->qhgd", d_scores, key_part, preferred_element_type=jnp.float32)
            * score_scale
        )
        d_key = (
            jnp.einsum(
                "hgqk,qhgd->khd", d_scores, query_grouped, preferred_element_type=jnp.float32
            )
            * score_scale
        )
        d_value = jnp.einsum(
            "hgqk,qhgd->khd", probs_low, d_attended, preferred_element_type=jnp.float32
        )
        return (d_query, (d_key, d_value))

    d_query, (d_key_blocks, d_value_blocks) = lax.scan(
        grad_step, start_total, (key_blocks, value_blocks, key_places)
    )
    d_key_all = d_key_blocks.reshape(seq_length, k_cols)
    d_value_all = d_value_blocks.reshape(seq_length, k_cols)
    d_key_own, d_value_own = (
        lax.psum_scatter(
            d_key_all.astype(jnp.bfloat16), "ctx", scatter_dimension=0, tiled=True
        ).astype(jnp.float32),
        lax.psum_scatter(
            d_value_all.astype(jnp.bfloat16), "ctx", scatter_dimension=0, tiled=True
        ).astype(jnp.float32),
    )

    def turn_back(grads):
        return jax.vjp(lambda values: rotate(values, cosine, sine), grads)[1](grads)[0]

    d_query_raw = turn_back(d_query.reshape(token_count, query_heads, head_dim)).reshape(
        token_count, q_cols
    )
    d_key_raw = turn_back(d_key_own.reshape(token_count, kv_heads, head_dim)).reshape(
        token_count, k_cols
    )
    d_mixed = jnp.concatenate([d_query_raw, d_key_raw, d_value_own], axis=1).astype(jnp.bfloat16)
    qkv_grad = jnp.dot(normed_one.T, d_mixed, preferred_element_type=jnp.float32)
    bias_grad = jnp.sum(d_mixed.astype(jnp.float32), axis=0)
    qk_bias_grad = bias_grad[: q_cols + k_cols]
    value_bias_grad = bias_grad[q_cols + k_cols :]
    d_normed_one = jnp.dot(d_mixed, qkv_full.T, preferred_element_type=jnp.float32)
    norm_one_back = jax.vjp(rms_apply, inputs_wide, gain_one_wide)[1]
    d_input_part, gain_one_grad = norm_one_back(d_normed_one)
    input_grad = (d_input_part + d_residual).astype(jnp.bfloat16)
    local_grads = (
        gain_one_grad,
        qkv_grad,
        qk_bias_grad,
        value_bias_grad,
        out_grad,
        gain_two_grad,
        gate_grad,
        up_grad,
        down_grad,
    )
    shard_grads = (
        lax.psum_scatter(
            local_grads[0].astype(jnp.bfloat16), "dp", scatter_dimension=0, tiled=True
        ).astype(jnp.float32),
        lax.psum_scatter(
            local_grads[1].astype(jnp.bfloat16), "dp", scatter_dimension=0, tiled=True
        ).astype(jnp.float32),
        lax.psum_scatter(
            local_grads[2].astype(jnp.bfloat16), "dp", scatter_dimension=0, tiled=True
        ).astype(jnp.float32),
        lax.psum_scatter(
            local_grads[3].astype(jnp.bfloat16), "dp", scatter_dimension=0, tiled=True
        ).astype(jnp.float32),
        lax.psum_scatter(
            local_grads[4].astype(jnp.bfloat16), "dp", scatter_dimension=0, tiled=True
        ).astype(jnp.float32),
        lax.psum_scatter(
            local_grads[5].astype(jnp.bfloat16), "dp", scatter_dimension=0, tiled=True
        ).astype(jnp.float32),
        lax.psum_scatter(
            local_grads[6].astype(jnp.bfloat16), "dp", scatter_dimension=0, tiled=True
        ).astype(jnp.float32),
        lax.psum_scatter(
            local_grads[7].astype(jnp.bfloat16), "dp", scatter_dimension=0, tiled=True
        ).astype(jnp.float32),
        lax.psum_scatter(
            local_grads[8].astype(jnp.bfloat16), "dp", scatter_dimension=0, tiled=True
        ).astype(jnp.float32),
    )
    summed = (
        lax.psum(shard_grads[0].astype(jnp.bfloat16), "ctx").astype(jnp.float32),
        lax.psum(shard_grads[1].astype(jnp.bfloat16), "ctx").astype(jnp.float32),
        lax.psum(shard_grads[2].astype(jnp.bfloat16), "ctx").astype(jnp.float32),
        lax.psum(shard_grads[3].astype(jnp.bfloat16), "ctx").astype(jnp.float32),
        lax.psum(shard_grads[4].astype(jnp.bfloat16), "ctx").astype(jnp.float32),
        lax.psum(shard_grads[5].astype(jnp.bfloat16), "ctx").astype(jnp.float32),
        lax.psum(shard_grads[6].astype(jnp.bfloat16), "ctx").astype(jnp.float32),
        lax.psum(shard_grads[7].astype(jnp.bfloat16), "ctx").astype(jnp.float32),
        lax.psum(shard_grads[8].astype(jnp.bfloat16), "ctx").astype(jnp.float32),
    )
    return (
        output,
        input_grad,
        summed[0],
        summed[1],
        summed[2],
        summed[3],
        summed[4],
        summed[5],
        summed[6],
        summed[7],
        summed[8],
    )


def solution(mesh):
    placed = (
        P(("dp", "ctx"), None),
        P(("dp", "ctx"), None),
        P(),
        P(("dp", "ctx")),
        P("dp"),
        P("dp", None),
        P("dp"),
        P("dp", None),
        P("dp"),
        P("dp", None),
        P("dp", None),
        P("dp", None),
    )
    return jax.shard_map(
        body,
        mesh=mesh,
        in_specs=placed,
        out_specs=(
            P(("dp", "ctx"), None),
            P(("dp", "ctx"), None),
            P("dp"),
            P("dp", None),
            P("dp"),
            P("dp"),
            P("dp", None),
            P("dp"),
            P("dp", None),
            P("dp", None),
            P("dp", None),
        ),
        check_vma=False,
    )
```

profile of v0, /device:TPU:1, one launch (start us, length us, event | category | flops | bytes accessed | tf_op | source)
XLA Modules:
  0.0 1149.3 jit_solution(3470323007845369848)
XLA Ops:
  13.2 9.4 all-reduce.14
  23.7 19.9 %all-gather.8.cloned.1.call-done = bf16[896,1152]{1,0:T(8,128)(2,1)} async-done(((bf16[224,1152]{1,0:T(8,128)(2,1)}), bf16[896,1152]{1,0:T(8,128)(2,1)}) %all-gather.8.cloned.1.call-update) | async-done | bytes 2064400 | tf_op jit(solution)/shard_map/all_gather | solution.py:84
  51.1 38.8 %all-gather.10.cloned.1.call-done = bf16[4096,128]{1,0:T(8,128)(2,1)} async-done(((bf16[128,128]{1,0:T(8,128)(2,1)}), bf16[4096,128]{1,0:T(8,128)(2,1)}) %all-gather.10.cloned.1.call-update) | async-done | bytes 1048592 | tf_op jit(solution)/shard_map/all_gather | solution.py:109
  89.9 5.0 reshape.338
  94.9 5.9 copy.88
  100.7 34.2 %all-gather.12.cloned.1.call-done = bf16[4096,128]{1,0:T(8,128)(2,1)} async-done(((bf16[128,128]{1,0:T(8,128)(2,1)}), bf16[4096,128]{1,0:T(8,128)(2,1)}) %all-gather.12.cloned.1.call-update) | async-done | bytes 1048592 | tf_op jit(solution)/shard_map/all_gather | solution.py:108
  134.9 5.0 reshape.339
  139.9 4.6 copy.89
  144.5 37.0 %while.39 = (s32[]{:T(128)}, f32[2,7,128]{2,1,0:T(8,128)S(1)}, f32[2,7,128]{2,1,0:T(8,128)S(1)}, s32[4,1024]{1,0:T(4,128)S(1)}, s32[128]{0:T(128)S(1)}, /*index=...) while((s32[]{:T(128)}, f32[2,7,128]{2,1,0:T(8,128)S(1)}, ...), condition=%wide.region_6.7_spmd.clone, body=%wide.region_3.6_spmd.clone.sunk | while | flops 247866112 | bytes 15670904 | solution.py:136
  144.8 4.1 fusion.161
  148.9 4.6 exponential_reduce_fusion.2
  153.7 4.1 fusion.161
  157.9 4.6 exponential_reduce_fusion.2
  162.7 4.1 fusion.161
  166.8 4.6 exponential_reduce_fusion.2
  171.7 4.7 fusion.161
  176.3 5.2 exponential_reduce_fusion.2
  181.6 14.9 %while.40 = (s32[]{:T(128)}, f32[128,2,7,64]{0,3,2,1:T(8,128)S(1)}, bf16[4,1024,2,64]{1,3,2,0:T(8,128)(2,1)}, s32[4,1024]{1,0:T(4,128)S(1)}, s32[128]{0:T(128)S(...) while((s32[]{:T(128)}, f32[128,2,7,64]{0,3,2,1:T(8,128)S(1)}, ...), condition=%wide.region_8.9_spmd.clone, body=%wide.region_7.8_spmd.clone.sunk | while | flops 477462528 | bytes 1955962 | solution.py:153
  181.8 3.4 fusion.167
  185.5 3.4 fusion.167
  189.2 3.4 fusion.167
  192.8 3.4 fusion.167
  199.6 49.8 %all-gather.16.cloned.1.call-done = bf16[896,4864]{1,0:T(8,128)(2,1)} async-done(((bf16[224,4864]{1,0:T(8,128)(2,1)}), bf16[896,4864]{1,0:T(8,128)(2,1)}) %all-gather.16.cloned.1.call-update) | async-done | bytes 8716304 | tf_op jit(solution)/shard_map/all_gather | solution.py:158
  249.4 6.4 fusion.102
  255.8 81.9 %all-gather.18.cloned.1.call-done = bf16[896,4864]{1,0:T(8,128)(2,1)} async-done(((bf16[224,4864]{1,0:T(8,128)(2,1)}), bf16[896,4864]{1,0:T(8,128)(2,1)}) %all-gather.18.cloned.1.call-update) | async-done | bytes 8716304 | tf_op jit(solution)/shard_map/all_gather | solution.py:159
  337.7 6.4 fusion.103
  344.1 82.1 %all-gather.20.cloned.1.call-done = bf16[4864,896]{1,0:T(8,128)(2,1)} async-done(((bf16[1216,896]{1,0:T(8,128)(2,1)}), bf16[4864,896]{1,0:T(8,128)(2,1)}) %all-gather.20.cloned.1.call-update) | async-done | bytes 8716304 | tf_op jit(solution)/shard_map/all_gather | solution.py:160
  426.3 7.5 multiply_convert_fusion
  433.8 7.2 fusion.104
  441.1 2.9 multiply_reduce_fusion
  449.2 71.4 %while.41 = (s32[]{:T(128)}, f32[128,2,7,64]{0,3,2,1:T(8,128)S(1)}, bf16[4,1024,2,64]{1,3,2,0:T(8,128)(2,1)}, bf16[4,1024,2,64]{1,3,2,0:T(8,128)(2,1)}, bf16[4,1...) while((s32[]{:T(128)}, f32[128,2,7,64]{0,3,2,1:T(8,128)S(1)}, ...), condition=%wide.region_12.13_spmd.clone, body=%wide.region_11.12_spmd.clone.sunk | while | flops 1193361408 | bytes 99781520 | solution.py:217
  450.8 5.4 fusion.179
  456.3 3.0 fusion.180
  460.9 5.2 fusion.182
  468.6 5.4 fusion.179
  474.0 3.0 fusion.180
  478.7 5.2 fusion.182
  486.4 5.4 fusion.179
  491.8 3.0 fusion.180
  496.5 5.2 fusion.182
  504.2 5.4 fusion.179
  509.6 3.0 fusion.180
  514.3 5.2 fusion.182
  520.6 6.0 copy.124
  526.5 4.7 reshape.332
  531.4 6.0 copy.123
  537.4 4.7 reshape.330
  544.2 64.3 %reduce-scatter.24.cloned.1.call-done = bf16[128,128]{1,0:T(8,128)(2,1)} async-done(((bf16[4096,128]{1,0:T(8,128)(2,1)}), bf16[128,128]{1,0:T(8,128)(2,1)}) %reduce-scatter.24.cloned.1.call-update) | async-done | bytes 32784
  609.3 80.0 %reduce-scatter.22.cloned.1.call-done = bf16[128,128]{1,0:T(8,128)(2,1)} async-done(((bf16[4096,128]{1,0:T(8,128)(2,1)}), bf16[128,128]{1,0:T(8,128)(2,1)}) %reduce-scatter.22.cloned.1.call-update) | async-done | bytes 32784
  692.7 7.2 convolution_convert_fusion.2
  699.9 7.2 convolution_convert_fusion.1
  708.1 4.7 convolution_convert_fusion
  712.9 5.3 reduce-scatter.14.cloned.1.call-done
  718.2 32.9 %reduce-scatter.12.cloned.1.call-done = bf16[224,1152]{1,0:T(8,128)(2,1)} async-done(((bf16[896,1152]{1,0:T(8,128)(2,1)}), bf16[224,1152]{1,0:T(8,128)(2,1)}) %reduce-scatter.12.cloned.1.call-update) | async-done | bytes 516112 | tf_op jit(solution)/shard_map/reduce_scatter | solution.py:264
  751.1 85.4 %reduce-scatter.16.cloned.1.call-done = bf16[224,4864]{1,0:T(8,128)(2,1)} async-done(((bf16[896,4864]{1,0:T(8,128)(2,1)}), bf16[224,4864]{1,0:T(8,128)(2,1)}) %reduce-scatter.16.cloned.1.call-update) | async-done | bytes 2179088 | tf_op jit(solution)/shard_map/reduce_scatter | solution.py:279
  836.5 85.4 %reduce-scatter.18.cloned.1.call-done = bf16[224,4864]{1,0:T(8,128)(2,1)} async-done(((bf16[896,4864]{1,0:T(8,128)(2,1)}), bf16[224,4864]{1,0:T(8,128)(2,1)}) %reduce-scatter.18.cloned.1.call-update) | async-done | bytes 2179088 | tf_op jit(solution)/shard_map/reduce_scatter | solution.py:282
  921.9 85.4 %reduce-scatter.20.cloned.1.call-done = bf16[1216,896]{1,0:T(8,128)(2,1)} async-done(((bf16[4864,896]{1,0:T(8,128)(2,1)}), bf16[1216,896]{1,0:T(8,128)(2,1)}) %reduce-scatter.20.cloned.1.call-update) | async-done | bytes 2179088 | tf_op jit(solution)/shard_map/reduce_scatter | solution.py:285
  1009.3 5.8 fusion.65
  1016.2 7.1 all-reduce.13
  1023.5 65.1 %all-reduce.11 = (bf16[224]{0:T(256)(128)(2,1)S(1)}, bf16[256]{0:T(256)(128)(2,1)S(1)}, bf16[32]{0:T(256)(128)(2,1)S(1)}, bf16[224]{0:T(256)(128)(2,1)S(1)}) all-reduce(bf16[224]{0:T(256)(128)(2,1)S(1)} %dynamic-slice.4, bf16[256]{0:T(256)(128)(2,1)S(1)} %dynamic-slice.6, ...), channel_id=1, replica_groups=mesh['dp'=4,'ctx'=32] {'ctx'}, use_global_device_ids=true, to_apply=%region_18.19 | all-reduce | flops 736 | bytes 2944 | tf_op jit(solution)/shard_map/psum | solution.py:290
  1091.7 39.1 %all-reduce.17.cloned.1.call-done = (bf16[224,1152]{1,0:T(8,128)(2,1)}, bf16[224,896]{1,0:T(8,128)(2,1)}, bf16[224,4864]{1,0:T(8,128)(2,1)}, bf16[224,4864]{1,0:T(8,128)(2,1)}, bf16[1216,896]{1,0:T(8,128)(2,1)}) async-done(((bf16[224,1152]{1,0:T(8,128)(2,1)}, bf16[224,896]{1,0:T(8,128)(2,1)}, bf16[224,4864]{1,0:T(8,128)(2,1)}, bf16[224,4864]{1,0:T(8,128)(2,1)}, bf16[1216,896]{1,0:T(8,128)(2,1)}), ...) | async-done | bytes 7454736 | tf_op jit(solution)/shard_map/psum | solution.py:291
  1135.1 2.3 convert_element_type.199
  1137.5 2.3 convert_element_type.201
  1140.0 2.3 convert_element_type.203
  (267 shorter events, 55.6 us)
Async XLA Ops:
  7.2 39.3 %copy-start.31 = (s32[128]{0:T(128)S(1)}, s32[128]{0:T(128)}, u32[]{:S(2)}) copy-start(s32[128]{0:T(128)} %param.21) | copy-start | bytes 1540
  7.2 36.4 %all-gather.8.cloned.1.call-start = ((), (), s32[]{:S(2)}) async-start(), calls=%async_computation.7 | async-start | bytes 2580480 | tf_op jit(solution)/shard_map/all_gather | solution.py:84
  7.9 82.0 %all-gather.10.cloned.1.call-start = ((), (), s32[]{:S(2)}) async-start(), calls=%async_computation.8 | async-start | bytes 1081344 | tf_op jit(solution)/shard_map/all_gather | solution.py:109
  23.7 23.3 %copy-start.29 = (f32[128]{0:T(128)}, f32[128]{0:T(128)S(1)}, u32[]{:S(2)}) copy-start(f32[128]{0:T(128)S(1)} %fusion.73) | copy-start | bytes 1540
  46.5 88.4 %all-gather.12.cloned.1.call-start = ((), (), s32[]{:S(2)}) async-start(), calls=%async_computation.9 | async-start | bytes 1081344 | tf_op jit(solution)/shard_map/all_gather | solution.py:108
  47.0 3.4 copy-start.28
  47.7 148.8 %all-gather.14.cloned.1.call-start = ((), (), s32[]{:S(2)}) async-start(), calls=%async_computation.10 | async-start | bytes 2007040 | tf_op jit(solution)/shard_map/all_gather | solution.py:86
  48.3 201.1 %all-gather.16.cloned.1.call-start = ((), (), s32[]{:S(2)}) async-start(), calls=%async_computation.11 | async-start | bytes 10895360 | tf_op jit(solution)/shard_map/all_gather | solution.py:158
  48.9 288.8 %all-gather.18.cloned.1.call-start = ((), (), s32[]{:S(2)}) async-start(), calls=%async_computation.12 | async-start | bytes 10895360 | tf_op jit(solution)/shard_map/all_gather | solution.py:159
  49.5 376.8 %all-gather.20.cloned.1.call-start = ((), (), s32[]{:S(2)}) async-start(), calls=%async_computation.13 | async-start | bytes 10895360 | tf_op jit(solution)/shard_map/all_gather | solution.py:160
  50.2 558.2 %reduce-scatter.24.cloned.1.call-start = ((), (), s32[]{:S(2)}) async-start(), calls=%async_computation.20 | async-start | bytes 1081344
  181.5 15.0 %copy-start.9 = (bf16[128,896]{1,0:T(8,128)(2,1)S(1)}, bf16[128,896]{1,0:T(8,128)(2,1)}, u32[]{:S(2)}) copy-start(bf16[128,896]{1,0:T(8,128)(2,1)} %param.18) | copy-start | bytes 688132
  196.4 59.3 %copy-start.19 = (f32[128,2,7,64]{0,3,2,1:T(8,128)}, f32[128,2,7,64]{0,3,2,1:T(8,128)S(1)}, u32[]{:S(2)}) copy-start(f32[128,2,7,64]{0,3,2,1:T(8,128)S(1)} %get-tuple-element.157) | copy-start | bytes 1376260
  196.5 59.3 %copy-start.17 = (bf16[128,2,7,64]{0,3,2,1:T(8,128)(2,1)}, bf16[128,2,7,64]{0,3,2,1:T(8,128)(2,1)S(1)}, u32[]{:S(2)}) copy-start(bf16[128,2,7,64]{0,3,2,1:T(8,128)(2,1)S(1)} %convert_element_type.171) | copy-start | bytes 688132
  433.8 7.2 copy-start.12
  433.8 7.2 copy-start.11
  433.8 7.2 copy-start.2
  433.8 7.2 copy-start.4
  441.1 2.9 copy-start.24
  441.1 3.9 copy-start.8
  449.4 1.4 copy-start.26
  450.6 5.7 copy-start.1
  456.2 3.1 copy-start
  456.2 3.4 copy-start.20
  456.2 4.7 copy-start.22
  456.2 4.7 copy-start.27
  460.9 5.3 copy-start.21
  467.2 1.4 copy-start.26
  468.4 5.7 copy-start.1
  474.0 3.1 copy-start
  474.0 3.4 copy-start.20
  474.0 4.7 copy-start.22
  474.0 4.7 copy-start.27
  478.7 5.3 copy-start.21
  485.0 1.4 copy-start.26
  486.1 5.7 copy-start.1
  491.8 3.1 copy-start
  491.8 3.4 copy-start.20
  491.8 4.7 copy-start.22
  491.8 4.7 copy-start.27
  496.5 5.3 copy-start.21
  502.8 1.4 copy-start.26
  503.9 5.7 copy-start.1
  509.6 3.1 copy-start
  509.6 3.4 copy-start.20
  509.6 4.7 copy-start.22
  509.6 4.7 copy-start.27
  514.3 5.3 copy-start.21
  531.3 158.0 %reduce-scatter.22.cloned.1.call-start = ((), (), s32[]{:S(2)}) async-start(), calls=%async_computation.19 | async-start | bytes 1081344
  531.3 10.9 copy-start.7
  531.3 10.9 copy-start.18
  542.2 148.1 %copy-start.10 = (bf16[128,896]{1,0:T(8,128)(2,1)S(1)}, bf16[128,896]{1,0:T(8,128)(2,1)}, u32[]{:S(2)}) copy-start(bf16[128,896]{1,0:T(8,128)(2,1)} %param.18) | copy-start | bytes 688132
  542.2 176.0 %reduce-scatter.14.cloned.1.call-start = ((), (), s32[]{:S(2)}) async-start(), calls=%async_computation.15 | async-start | bytes 2007040 | tf_op jit(solution)/shard_map/reduce_scatter | solution.py:273
  544.0 207.1 %reduce-scatter.12.cloned.1.call-start = ((), (), s32[]{:S(2)}) async-start(), calls=%async_computation.14 | async-start | bytes 2580480 | tf_op jit(solution)/shard_map/reduce_scatter | solution.py:264
  692.4 144.1 %reduce-scatter.16.cloned.1.call-start = ((), (), s32[]{:S(2)}) async-start(), calls=%async_computation.16 | async-start | bytes 10895360 | tf_op jit(solution)/shard_map/reduce_scatter | solution.py:279
  699.9 222.0 %reduce-scatter.18.cloned.1.call-start = ((), (), s32[]{:S(2)}) async-start(), calls=%async_computation.17 | async-start | bytes 10895360 | tf_op jit(solution)/shard_map/reduce_scatter | solution.py:282
  707.1 300.1 %reduce-scatter.20.cloned.1.call-start = ((), (), s32[]{:S(2)}) async-start(), calls=%async_computation.18 | async-start | bytes 10895360 | tf_op jit(solution)/shard_map/reduce_scatter | solution.py:285
  712.8 418.0 %all-reduce.17.cloned.1.call-start = ((), (), s32[]{:S(2)}) async-start(), calls=%async_computation.21 | async-start | bytes 14909440 | tf_op jit(solution)/shard_map/psum | solution.py:291
  1007.2 2.0 copy-start.5
  1009.3 6.0 copy-start.16
  1015.1 75.8 %copy-start.30 = (f32[128]{0:T(128)S(1)}, f32[128]{0:T(128)}, u32[]{:S(2)}) copy-start(f32[128]{0:T(128)} %copy-done.29) | copy-start | bytes 1540
  1130.8 4.3 copy-start.15
  1133.0 4.4 copy-start.14
  1137.5 2.5 copy-start.13
  (7 other events, 6.5 us)
Sparse Core Ops, SparseCore 0:
  9.7 33.8 all-gather.7
  46.6 43.2 all-gather.9
  92.8 42.0 all-gather.11
  136.4 25.5 all-gather.13
  163.5 85.8 all-gather.15
  250.9 86.7 all-gather.17
  339.4 86.8 all-gather.19
  531.4 77.0 reduce-scatter.23
  612.4 76.8 reduce-scatter.21
  692.1 26.0 reduce-scatter.13
  721.2 29.8 reduce-scatter.11
  753.6 82.8 reduce-scatter.15
  839.0 82.8 reduce-scatter.17
  924.3 82.8 reduce-scatter.19
  1011.3 119.5 all-reduce.16
where the time goes:
time: 1160 us; the launch traced here: 1150 us
  waiting for transfers between devices  788 us (68%)
  matrix products  160 us (14%)
  blocking collectives  81.5 us (7%)
  local copies, waits for them, and re-layouts  59.3 us (5%)
  other arithmetic  40.1 us (3%)
  between operations  18.4 us (2%)
    unnamed x17, waiting for transfers between devices  147 us
    reduce_scatter x1, waiting for transfers between devices, body(): lax.psum_scatter(local_grads[6].astype(jnp.bfloat16), 'dp', scatter_dimen...  85.4 us
    reduce_scatter x1, waiting for transfers between devices, body(): lax.psum_scatter(local_grads[8].astype(jnp.bfloat16), 'dp', scatter_dimen...  85.4 us
    reduce_scatter x1, waiting for transfers between devices, body(): lax.psum_scatter(local_grads[7].astype(jnp.bfloat16), 'dp', scatter_dimen...  85.4 us
    all_gather x1, waiting for transfers between devices, body(): lax.all_gather(down_weight, 'dp', axis=0, tiled=True)  82.1 us
    all_gather x1, waiting for transfers between devices, body(): lax.all_gather(up_weight, 'dp', axis=0, tiled=True)  81.9 us
    psum x1, blocking collectives, body(): lax.psum(shard_grads[0].astype(jnp.bfloat16), 'ctx').astype(jnp.float32)  65.1 us
    all_gather x1, waiting for transfers between devices, body(): lax.all_gather(gate_weight, 'dp', axis=0, tiled=True)  49.8 us
  transfers between devices with their start and end apart: 15, of which 14 were waited for; matrix products, arithmetic and copies ran while one was open for 12% of the time, Pallas kernels for 0%

commit v1 on v0

v1 whole, which is shorter than its diff:
```python
import functools

import jax
import jax.numpy as jnp
from jax import lax
from jax.experimental import pallas as pl
from jax.experimental.pallas import tpu as pltpu
from jax.sharding import Mesh, PartitionSpec as P

QH = 14
KVH = 2
HD = 64
GROUP = QH // KVH
D = 896
FF = 4864
SPAN = 64
CHUNK = 256

norm_eps = 1e-06
rope_base = 1000000.0
masked_score = -1e30
CTX = ("z", "y", "core")


def rms_apply(values, gain):
    mean_square = jnp.mean(values * values, axis=-1, keepdims=True)
    return values * lax.rsqrt(mean_square + norm_eps) * gain


def half_turn(values):
    middle = values.shape[-1] // 2
    return jnp.concatenate([-values[..., middle:], values[..., :middle]], axis=-1)


def rotate(values, cosine, sine):
    return values * cosine + half_turn(values) * sine


def rope_tables(positions, head_dim):
    middle = head_dim // 2
    inverse = rope_base ** (-(jnp.arange(middle).astype(jnp.float32) * 2.0) / head_dim)
    angles = positions.astype(jnp.float32)[:, None] * inverse[None, :]
    angles = jnp.concatenate([angles, angles], axis=-1)
    return (jnp.cos(angles), jnp.sin(angles))


def swiglu(gate_in, up_in):
    return jax.nn.silu(gate_in) * up_in


def dot(a, b, ca=1, cb=0):
    return lax.dot_general(a, b, (((ca,), (cb,)), ((), ())), preferred_element_type=jnp.float32)


def causal_copy(order_ref, kv_ref, sorted_ref):
    def move(slot, unused):
        source = pl.multiple_of(slot * SPAN, SPAN)
        target = pl.multiple_of(order_ref[slot] * SPAN, SPAN)
        sorted_ref[pl.ds(target, SPAN), :] = kv_ref[pl.ds(source, SPAN), :]
        return unused

    lax.fori_loop(0, kv_ref.shape[0] // SPAN, move, 0)


def visible(start, place, rows):
    key_place = lax.broadcasted_iota(jnp.int32, (CHUNK, rows), 0) + start
    lane = lax.broadcasted_iota(jnp.int32, (CHUNK, rows), 1)
    return key_place <= place * SPAN + lane % SPAN


def attend_kernel(order_ref, mine_ref, kv_ref, q_ref, out_ref, lse_ref, sorted_ref):
    causal_copy(order_ref, kv_ref, sorted_ref)
    rows = q_ref.shape[-1]
    for half in range(2):
        place = mine_ref[half]
        last = place * SPAN // CHUNK

        def step(index, carry, masked, half=half, place=place):
            start = pl.multiple_of(index * CHUNK, CHUNK)
            keys = sorted_ref[pl.ds(start, CHUNK), :128]
            values = sorted_ref[pl.ds(start, CHUNK), 128:]
            result = []
            for head in range(KVH):
                top, total, mixed = carry[head]
                scores = dot(keys, q_ref[half, head])
                if masked:
                    scores = jnp.where(visible(start, place, rows), scores, masked_score)
                new_top = jnp.maximum(top, jnp.max(scores, axis=0, keepdims=True))
                shrink = jnp.exp(top - new_top)
                weights = jnp.exp(scores - new_top)
                total = total * shrink + jnp.sum(weights, axis=0, keepdims=True)
                mixed = mixed * shrink + dot(values, weights.astype(jnp.bfloat16), 0, 0)
                result.append((new_top, total, mixed))
            return tuple(result)

        empty = tuple(
            (
                jnp.full((1, rows), masked_score, jnp.float32),
                jnp.zeros((1, rows), jnp.float32),
                jnp.zeros((128, rows), jnp.float32),
            )
            for head in range(KVH)
        )
        carry = lax.fori_loop(0, last, functools.partial(step, masked=False), empty)
        carry = step(last, carry, True)
        for head in range(KVH):
            top, total, mixed = carry[head]
            out_ref[half, head] = mixed[head * HD : (head + 1) * HD] / total
            lse_ref[half, head] = top + jnp.log(total)


def attend(order, mine, kv_all, q_pad):
    halves, heads, unused, rows = q_pad.shape
    smem = pl.BlockSpec(memory_space=pltpu.SMEM)
    vmem = pl.BlockSpec(memory_space=pltpu.VMEM)
    return pl.pallas_call(
        attend_kernel,
        out_shape=(
            jax.ShapeDtypeStruct((halves, heads, HD, rows), jnp.float32),
            jax.ShapeDtypeStruct((halves, heads, 1, rows), jnp.float32),
        ),
        in_specs=[smem, smem, vmem, vmem],
        out_specs=(vmem, vmem),
        scratch_shapes=[pltpu.VMEM(kv_all.shape, kv_all.dtype)],
        compiler_params=pltpu.CompilerParams(vmem_limit_bytes=48 * 1024 * 1024),
        cost_estimate=pl.CostEstimate(
            flops=3_000_000_000, bytes_accessed=6_000_000, transcendentals=4_000_000
        ),
        name="attend",
    )(order, mine, kv_all, q_pad)


def attend_back_kernel(
    order_ref,
    mine_ref,
    kv_ref,
    q_ref,
    q_rows_ref,
    do_ref,
    do_rows_ref,
    lse_ref,
    delta_ref,
    dq_ref,
    dkv_ref,
    sorted_ref,
    sum_ref,
):
    causal_copy(order_ref, kv_ref, sorted_ref)
    sum_ref[...] = jnp.zeros_like(sum_ref)
    rows = q_ref.shape[-1]
    for half in range(2):
        place = mine_ref[half]
        last = place * SPAN // CHUNK

        def step(index, carry, masked, half=half, place=place):
            start = pl.multiple_of(index * CHUNK, CHUNK)
            keys = sorted_ref[pl.ds(start, CHUNK), :128]
            values = sorted_ref[pl.ds(start, CHUNK), 128:]
            d_keys = sum_ref[pl.ds(start, CHUNK), :128]
            d_values = sum_ref[pl.ds(start, CHUNK), 128:]
            result = []
            for head in range(KVH):
                scores = dot(keys, q_ref[half, head])
                probs = jnp.exp(scores - lse_ref[half, head])
                if masked:
                    probs = jnp.where(visible(start, place, rows), probs, 0.0)
                d_probs = dot(values, do_ref[half, head])
                d_scores = (probs * (d_probs - delta_ref[half, head])).astype(jnp.bfloat16)
                d_values += dot(probs.astype(jnp.bfloat16), do_rows_ref[half, head])
                d_keys += dot(d_scores, q_rows_ref[half, head])
                result.append(carry[head] + dot(keys, d_scores, 0, 0))
            sum_ref[pl.ds(start, CHUNK), :128] = d_keys
            sum_ref[pl.ds(start, CHUNK), 128:] = d_values
            return tuple(result)

        empty = tuple(jnp.zeros((128, rows), jnp.float32) for head in range(KVH))
        carry = lax.fori_loop(0, last, functools.partial(step, masked=False), empty)
        carry = step(last, carry, True)
        for head in range(KVH):
            dq_ref[half, head] = carry[head][head * HD : (head + 1) * HD] * (HD**-0.5)

    def move(slot, unused):
        target = pl.multiple_of(slot * SPAN, SPAN)
        source = pl.multiple_of(order_ref[slot] * SPAN, SPAN)
        dkv_ref[pl.ds(target, SPAN), :] = sum_ref[pl.ds(source, SPAN), :].astype(jnp.bfloat16)
        return unused

    lax.fori_loop(0, dkv_ref.shape[0] // SPAN, move, 0)


def attend_back(order, mine, kv_all, q_pad, q_rows, do_pad, do_rows, lse, delta):
    halves, heads, unused, rows = q_pad.shape
    smem = pl.BlockSpec(memory_space=pltpu.SMEM)
    vmem = pl.BlockSpec(memory_space=pltpu.VMEM)
    return pl.pallas_call(
        attend_back_kernel,
        out_shape=(
            jax.ShapeDtypeStruct((halves, heads, HD, rows), jnp.float32),
            jax.ShapeDtypeStruct(kv_all.shape, jnp.bfloat16),
        ),
        in_specs=[smem, smem] + [vmem] * 7,
        out_specs=(vmem, vmem),
        scratch_shapes=[
            pltpu.VMEM(kv_all.shape, kv_all.dtype),
            pltpu.VMEM(kv_all.shape, jnp.float32),
        ],
        compiler_params=pltpu.CompilerParams(vmem_limit_bytes=48 * 1024 * 1024),
        cost_estimate=pl.CostEstimate(
            flops=8_000_000_000, bytes_accessed=9_000_000, transcendentals=4_000_000
        ),
        name="attend_back",
    )(order, mine, kv_all, q_pad, q_rows, do_pad, do_rows, lse, delta)


def split_rows(tokens):
    parts = tokens.reshape(2, SPAN, KVH, GROUP, HD)
    return parts.transpose(0, 2, 3, 1, 4).reshape(2, KVH, GROUP * SPAN, HD)


def pad_heads(rows):
    return jnp.stack(
        [
            jnp.pad(rows[:, 0], ((0, 0), (0, 0), (0, HD))),
            jnp.pad(rows[:, 1], ((0, 0), (0, 0), (HD, 0))),
        ],
        axis=1,
    )


def join_rows(columns):
    parts = columns.reshape(2, KVH, HD, GROUP, SPAN)
    return parts.transpose(0, 4, 1, 3, 2).reshape(2 * SPAN, QH * HD)


def body(
    inputs,
    cotangent,
    span_order,
    positions,
    attn_gain,
    qkv_weight,
    qkv_bias,
    out_weight,
    mlp_gain,
    gate_weight,
    up_weight,
    down_weight,
):
    token_count = inputs.shape[0]
    q_cols = QH * HD
    k_cols = KVH * HD
    slices = lax.axis_size("dp")
    own_rows = D // slices
    part = FF // (slices * 2)
    dp = lax.axis_index("dp")
    core = lax.axis_index("core")
    slot = (lax.axis_index("z") * lax.axis_size("y") + lax.axis_index("y")) * 2 + core

    qkv_full = lax.all_gather(qkv_weight, "dp", axis=0, tiled=True)
    small = lax.all_gather(jnp.concatenate([attn_gain, mlp_gain, qkv_bias]), "dp", axis=0)
    gain_one_wide = small[:, :own_rows].reshape(D).astype(jnp.float32)
    gain_two_wide = small[:, own_rows : 2 * own_rows].reshape(D).astype(jnp.float32)
    bias_full = small[:, 2 * own_rows :].reshape(-1).astype(jnp.float32)
    out_full = lax.all_gather(out_weight, "dp", axis=0, tiled=True)

    stacked = jnp.stack([gate_weight, up_weight])
    stacked = stacked.reshape(2, own_rows, slices, 2, part)
    stacked = lax.dynamic_index_in_dim(stacked, core, axis=3, keepdims=False)
    stacked = stacked.transpose(2, 0, 1, 3)
    received = lax.all_to_all(stacked, "dp", 0, 0, tiled=True)
    gate_part = received[:, 0].reshape(D, part)
    up_part = received[:, 1].reshape(D, part)
    down_part = lax.dynamic_slice_in_dim(down_weight, core * part, part, axis=0)
    cot_all = lax.all_gather(cotangent, ("dp", "core"), axis=0, tiled=True)

    inputs_wide = inputs.astype(jnp.float32)
    normed_one = rms_apply(inputs_wide, gain_one_wide).astype(jnp.bfloat16)
    mixed_proj = dot(normed_one, qkv_full) + bias_full
    cosine, sine = rope_tables(positions, HD)
    cosine = cosine[:, None, :]
    sine = sine[:, None, :]
    query_rot = rotate(
        mixed_proj[:, :q_cols].reshape(token_count, QH, HD), cosine, sine
    ).astype(jnp.bfloat16)
    key_rot = rotate(
        mixed_proj[:, q_cols : q_cols + k_cols].reshape(token_count, KVH, HD), cosine, sine
    )
    key_rot = key_rot.astype(jnp.bfloat16).reshape(token_count, k_cols)
    value_low = mixed_proj[:, q_cols + k_cols :].astype(jnp.bfloat16)
    kv_all = lax.all_gather(
        jnp.concatenate([key_rot, value_low], axis=1), CTX, axis=0, tiled=True
    )
    mine = lax.dynamic_slice_in_dim(span_order, 2 * slot, 2)
    q_rows = pad_heads(split_rows(query_rot * jnp.bfloat16(HD**-0.5)))
    q_pad = q_rows.transpose(0, 1, 3, 2)
    attended_cols, lse = attend(span_order, mine, kv_all, q_pad)
    attended_wide = join_rows(attended_cols)
    attended_low = attended_wide.astype(jnp.bfloat16)
    residual = inputs_wide + dot(attended_low, out_full)
    normed_two = rms_apply(residual, gain_two_wide).astype(jnp.bfloat16)

    normed_all = lax.all_gather(normed_two, ("dp", "core"), axis=0, tiled=True)
    gate_proj = dot(normed_all, gate_part)
    up_proj = dot(normed_all, up_part)
    hidden_low = swiglu(gate_proj, up_proj).astype(jnp.bfloat16)
    out_sum = dot(hidden_low, down_part).astype(jnp.bfloat16)
    d_hidden = dot(cot_all, down_part, 1, 1)
    d_gate, d_up = jax.vjp(swiglu, gate_proj, up_proj)[1](d_hidden)
    d_gate = d_gate.astype(jnp.bfloat16)
    d_up = d_up.astype(jnp.bfloat16)
    d_norm_sum = (dot(d_gate, gate_part, 1, 1) + dot(d_up, up_part, 1, 1)).astype(jnp.bfloat16)
    down_grad = dot(hidden_low, cot_all, 0, 0).astype(jnp.bfloat16)
    gate_grad = dot(normed_all, d_gate, 0, 0).astype(jnp.bfloat16)
    up_grad = dot(normed_all, d_up, 0, 0).astype(jnp.bfloat16)
    d_normed_two = lax.psum_scatter(
        d_norm_sum, ("dp", "core"), scatter_dimension=0, tiled=True
    ).astype(jnp.float32)
    output = (
        residual
        + lax.psum_scatter(out_sum, ("dp", "core"), scatter_dimension=0, tiled=True).astype(
            jnp.float32
        )
    ).astype(jnp.bfloat16)
    down_grad, gate_grad, up_grad = lax.psum((down_grad, gate_grad, up_grad), ("z", "y"))

    d_resid_part, gain_two_grad = jax.vjp(rms_apply, residual, gain_two_wide)[1](d_normed_two)
    d_residual = d_resid_part + cotangent.astype(jnp.float32)
    d_branch = d_residual.astype(jnp.bfloat16)
    d_attended = dot(d_branch, out_full, 1, 1).astype(jnp.bfloat16)
    row_delta = jnp.sum(
        (d_attended.astype(jnp.float32) * attended_wide).reshape(
            2, SPAN, KVH, GROUP, HD
        ),
        axis=-1,
    )
    row_delta = row_delta.transpose(0, 2, 3, 1).reshape(2, KVH, 1, GROUP * SPAN)
    do_rows = pad_heads(split_rows(d_attended))
    do_pad = do_rows.transpose(0, 1, 3, 2)
    d_query_cols, d_kv_all = attend_back(
        span_order, mine, kv_all, q_pad, q_rows, do_pad, do_rows, lse, row_delta
    )
    d_kv = lax.psum_scatter(d_kv_all, CTX, scatter_dimension=0, tiled=True).astype(jnp.float32)

    def turn_back(grads):
        scaled = grads * sine
        middle = HD // 2
        back = jnp.concatenate([scaled[..., middle:], -scaled[..., :middle]], axis=-1)
        return grads * cosine + back

    d_query_raw = turn_back(join_rows(d_query_cols).reshape(token_count, QH, HD))
    d_key_raw = turn_back(d_kv[:, :k_cols].reshape(token_count, KVH, HD))
    d_mixed = jnp.concatenate(
        [
            d_query_raw.reshape(token_count, q_cols),
            d_key_raw.reshape(token_count, k_cols),
            d_kv[:, k_cols:],
        ],
        axis=1,
    ).astype(jnp.bfloat16)

    def my_columns(tokens):
        parts = tokens.reshape(token_count, slices, own_rows).transpose(1, 0, 2)
        moved = lax.all_to_all(parts, "dp", 0, 0, tiled=True)
        return moved.reshape(slices * token_count, own_rows)

    normed_one_mine = my_columns(normed_one)
    attended_mine = my_columns(attended_low)
    d_branch_all = lax.all_gather(d_branch, "dp", axis=0, tiled=True)
    out_grad = dot(attended_mine, d_branch_all, 0, 0).astype(jnp.bfloat16)
    d_mixed_all = lax.all_gather(d_mixed, "dp", axis=0, tiled=True)
    qkv_grad = dot(normed_one_mine, d_mixed_all, 0, 0).astype(jnp.bfloat16)
    bias_grad = jnp.sum(d_mixed.astype(jnp.float32), axis=0)
    d_normed_one = dot(d_mixed, qkv_full, 1, 1)
    d_input_part, gain_one_grad = jax.vjp(rms_apply, inputs_wide, gain_one_wide)[1](d_normed_one)
    input_grad = (d_input_part + d_residual).astype(jnp.bfloat16)

    out_grad, qkv_grad = lax.psum((out_grad, qkv_grad), CTX)
    vectors = lax.psum(
        jnp.concatenate([gain_one_grad, gain_two_grad, bias_grad]), ("dp",) + CTX
    )

    def owned(start, count):
        width = count // slices
        return lax.dynamic_slice_in_dim(vectors, start + dp * width, width)

    gate_up = jnp.stack([gate_grad, up_grad]).reshape(2, slices, own_rows, part)
    gate_up = lax.all_to_all(gate_up.transpose(1, 0, 2, 3), "dp", 0, 0, tiled=True)
    gate_up = lax.all_gather(gate_up, "core", axis=1)
    gate_up = gate_up.transpose(2, 3, 0, 1, 4).reshape(2, own_rows, FF).astype(jnp.float32)
    down_grad = lax.all_gather(down_grad, "core", axis=0, tiled=True)
    return (
        output,
        input_grad,
        owned(0, D),
        qkv_grad.astype(jnp.float32),
        owned(2 * D, q_cols + k_cols),
        owned(2 * D + q_cols + k_cols, k_cols),
        out_grad.astype(jnp.float32),
        owned(D, D),
        gate_up[0],
        gate_up[1],
        down_grad.astype(jnp.float32),
    )


def solution(mesh):
    grid = Mesh(mesh.devices.reshape(4, 4, 4, 2), ("dp", "z", "y", "core"))
    tokens = ("dp",) + CTX
    return jax.shard_map(
        body,
        mesh=grid,
        in_specs=(
            P(tokens, None),
            P(tokens, None),
            P(),
            P(tokens),
            P("dp"),
            P("dp", None),
            P("dp"),
            P("dp", None),
            P("dp"),
            P("dp", None),
            P("dp", None),
            P("dp", None),
        ),
        out_specs=(
            P(tokens, None),
            P(tokens, None),
            P("dp"),
            P("dp", None),
            P("dp"),
            P("dp"),
            P("dp", None),
            P("dp"),
            P("dp", None),
            P("dp", None),
            P("dp", None),
        ),
        check_vma=False,
    )
```

time: 1160 us -> 724 us (0.62)
  waiting for transfers between devices: 788 us -> 335 us
  matrix products: 160 us -> 48.8 us
  local copies, waits for them, and re-layouts: 59.3 us -> 105 us
  blocking collectives: 81.5 us -> 114 us
  Pallas kernels: 0 us -> 31.8 us
  starting transfers between devices: 0.86 us -> 17.6 us
    all_gather x7 -> x8, waiting for transfers between devices: 307 us -> 70.1 us  [the longest x1 31.5 us: body(): lax.all_gather(jnp.concatenate([key_rot, value_low], axis=1), CTX, axis=0...]
    reduce_scatter x5 -> x3, waiting for transfers between devices: 294 us -> 83.1 us  [the longest x1 54.3 us: body(): lax.psum_scatter(d_kv_all, CTX, scatter_dimension=0, tiled=True)]
    unnamed x17 -> x13, waiting for transfers between devices: 147 us -> 1.85 us
    dot_general x43 -> x15, matrix products: 160 us -> 48.8 us  [dot(): lax.dot_general(a, b, (((ca,), (cb,)), ((), ())), preferred_element_type=...]
    psum x1 -> x2, waiting for transfers between devices: 39.1 us -> 136 us  [the longest x1 99.6 us: body(): lax.psum((down_grad, gate_grad, up_grad), ('z', 'y'))]
    all_to_all x0 -> x4, waiting for transfers between devices: none -> 44.2 us  [the longest x1 34.8 us: body(): received = lax.all_to_all(stacked, 'dp', 0, 0, tiled=True)]
    all_gather x0 -> x1, blocking collectives: none -> 36.1 us  [body(): d_branch_all = lax.all_gather(d_branch, 'dp', axis=0, tiled=True)]
    unnamed x67 -> x83, local copies, waits for them, and re-layouts: 40.5 us -> 8.42 us
  transfers between devices with their start and end apart: 15 -> 17, of which waited for: 14 -> 11; matrix products, arithmetic and copies ran while one was open for 12% -> 17% of each run, Pallas kernels for 0% -> 2%
where the time goes in v1:
time: 724 us; the launch traced here: 715 us
  waiting for transfers between devices  335 us (46%)
  blocking collectives  114 us (16%)
  local copies, waits for them, and re-layouts  105 us (15%)
  matrix products  48.8 us (7%)
  other arithmetic  47.1 us (7%)
  Pallas kernels  31.8 us (4%)
  starting transfers between devices  17.6 us (2%)
  between operations  15.7 us (2%)
    psum x1, waiting for transfers between devices, body(): lax.psum((down_grad, gate_grad, up_grad), ('z', 'y'))  99.6 us
    psum x1, blocking collectives, body(): lax.psum(jnp.concatenate([gain_one_grad, gain_two_grad, bias_grad]), ('dp...  69 us
    reduce_scatter x1, waiting for transfers between devices, body(): lax.psum_scatter(d_kv_all, CTX, scatter_dimension=0, tiled=True)  54.3 us
    dot_general x15, matrix products, dot(): lax.dot_general(a, b, (((ca,), (cb,)), ((), ())), preferred_element_type=...  48.8 us
    psum x1, waiting for transfers between devices, body(): out_grad, qkv_grad = lax.psum((out_grad, qkv_grad), CTX)  36.3 us
    all_gather x1, blocking collectives, body(): d_branch_all = lax.all_gather(d_branch, 'dp', axis=0, tiled=True)  36.1 us
    all_to_all x1, waiting for transfers between devices, body(): received = lax.all_to_all(stacked, 'dp', 0, 0, tiled=True)  34.8 us
    all_gather x1, waiting for transfers between devices, body(): lax.all_gather(jnp.concatenate([key_rot, value_low], axis=1), CTX, axis=0...  31.5 us
  transfers between devices with their start and end apart: 17, of which 11 were waited for; matrix products, arithmetic and copies ran while one was open for 17% of the time, Pallas kernels for 2%

profile of v1, /device:TPU:1, one launch (start us, length us, event | category | flops | bytes accessed | tf_op | source)
XLA Modules:
  0.0 715.2 jit_solution(15042212261812299052)
XLA Ops:
  10.9 9.4 %all-reduce.4 = bf16[2944]{0:T(1024)(128)(2,1)S(1)} all-reduce(bf16[2944]{0:T(1024)(128)(2,1)S(1)} %dynamic-update-slice), channel_id=2, replica_groups=mesh['dp'=4,'z'=4,'y'=4,'core'=2] {'dp'}, use_global_device_ids=true, to_apply=%add.4 | all-reduce | flops 2944 | bytes 11776
  24.4 19.0 %all-gather.11.cloned.1.call-done = bf16[896,1152]{1,0:T(8,128)(2,1)} async-done(((bf16[224,1152]{1,0:T(8,128)(2,1)}), bf16[896,1152]{1,0:T(8,128)(2,1)}) %all-gather.11.cloned.1.call-update) | async-done | bytes 2064400 | tf_op jit(solution)/shard_map/all_gather | solution.py:259
  43.5 2.1 convolution_add_fusion
  51.2 2.1 concatenate.57
  54.3 2.8 multiply_bitcast_fusion
  59.7 31.5 %all-gather.13.cloned.1.call-done.kv_ref = bf16[4096,256]{1,0:T(8,128)(2,1)} async-done(((bf16[128,256]{1,0:T(8,128)(2,1)}), bf16[4096,256]{1,0:T(8,128)(2,1)}) %all-gather.13.cloned.1.call-update) | async-done | bytes 2097168 | tf_op jit(solution)/shard_map/all_gather | solution.py:290
  91.2 1.6 copy-done.5
  92.8 15.4 %attend.1 = (f32[2,2,64,448]{3,2,1,0:T(8,128)S(1)}, f32[2,2,1,448]{3,2,1,0:T(1,128)S(1)}) custom-call(s32[64]{0:T(128)S(1)} %copy-done.6, s32[2]{0:T(128)S(1)} %dynamic_slice.22.mine_ref, bf16[4096,256]{1,0:T(8,128)(2,1)S(1)} %copy-done.5, bf16[2,2,128,448]{3,2,1,0:T(8,128)(2,1)S(1)} %copy.141.q_ref), custom_call_target="tpu_custom_call" | custom-call | flops 3000000000 | bytes 6000000 | tf_op jit(solution)/shard_map/attend/pallas_call | solution.py:116
  109.4 2.2 copy.143
  111.6 2.5 reshape.247
  114.1 4.4 all-gather.15.cloned.1.call-done
  118.4 2.1 multiply_reduce_fusion
  122.0 5.9 stack.40
  127.9 5.9 stack.39
  133.8 10.6 %dynamic-slice_maximum_fusion = bf16[2,224,4,1,608]{4,3,2,1,0:T(2,128)(2,1)} fusion(s32[]{:T(128)S(6)} %select_n.23, bf16[1,224,4,2,608]{4,3,2,1,0:T(2,128)(2,1)} %stack.40, bf16[1,224,4,2,608]{4,3,2,1,0:T(2,128)(2,1)} %stack.39), kind=kLoop, calls=%fused_computation.1 | loop fusion | flops 4358144 | bytes 6537220 | tf_op jit(solution)/shard_map/stack | solution.py:266
  144.4 4.1 copy.185
  148.5 4.5 all-to-all-start
  153.4 34.8 %all-to-all-done = bf16[4,2,224,608]{3,2,1,0:T(8,128)(2,1)} async-done(((bf16[4,2,224,608]{3,2,1,0:T(8,128)(2,1)}), bf16[4,2,224,608]{3,2,1,0:T(8,128)(2,1)}, u32[]{:S(2)}, u32[]{:S(2)}) %all-to-all-start) | async-done | bytes 2179104 | tf_op jit(solution)/shard_map/all_to_all | solution.py:270
  188.2 3.2 fusion.41
  191.5 4.9 fusion.45
  196.4 3.0 fusion.46
  199.4 6.5 fusion.3
  205.9 1.8 fusion.47
  208.0 3.1 add_convert_fusion
  211.1 2.0 copy.149
  213.1 28.8 %reduce-scatter.6.cloned.1.call-done = bf16[128,896]{1,0:T(8,128)(2,1)} async-done(((bf16[1024,896]{1,0:T(8,128)(2,1)}), bf16[128,896]{1,0:T(8,128)(2,1)}) %reduce-scatter.6.cloned.1.call-update) | async-done | bytes 229392 | tf_op jit(solution)/shard_map/reduce_scatter | solution.py:315
  241.9 1.8 fusion.17
  245.0 2.5 convert_multiply_fusion.6
  251.2 2.0 copy.153.do_ref
  254.2 2.5 reshape.250
  261.4 16.4 %attend_back.1 = (f32[2,2,64,448]{3,2,1,0:T(8,128)S(1)}, bf16[4096,256]{1,0:T(8,128)(2,1)S(1)}) custom-call(s32[64]{0:T(128)S(1)} %copy-done.6, s32[2]{0:T(128)S(1)} %dynamic_slice.22.mine_ref, bf16[4096,256]{1,0:T(8,128)(2,1)} %all-gather.13.cloned.1.call-done.kv_ref, bf16[2,2,128,448]{3,2,1,0:T(8,128)(2,1)S(1)} %copy.141.q_ref, ...), custom_call_target="tpu_custom_call" | custom-call | flops 8000000000 | bytes 9000000 | tf_op jit(solution)/shard_map/attend_back/pallas_call | solution.py:195
  279.2 4.3 convolution_convert_fusion.2
  283.5 2.4 copy.167
  285.8 4.3 convolution_convert_fusion.3
  290.2 2.4 copy.166
  292.5 4.4 convolution_convert_fusion.4
  298.2 2.0 copy.155
  304.1 54.3 %reduce-scatter.8.cloned.1.call-done = bf16[128,256]{1,0:T(8,128)(2,1)} async-done(((bf16[4096,256]{1,0:T(8,128)(2,1)}), bf16[128,256]{1,0:T(8,128)(2,1)}) %reduce-scatter.8.cloned.1.call-update) | async-done | bytes 65552 | tf_op jit(solution)/shard_map/reduce_scatter | solution.py:342
  361.3 99.6 %all-reduce.12.cloned.1.call-done = (bf16[1,4,224,608]{3,2,1,0:T(8,128)(2,1)}, bf16[1,4,224,608]{3,2,1,0:T(8,128)(2,1)}, bf16[608,896]{1,0:T(8,128)(2,1)}) async-done(((bf16[1,4,224,608]{3,2,1,0:T(8,128)(2,1)}, bf16[1,4,224,608]{3,2,1,0:T(8,128)(2,1)}, bf16[608,896]{1,0:T(8,128)(2,1)}), (bf16[1,4,224,608]{3,2,1,0:T(8,128)(2,1)}, bf16[1,4,224,608]{3,2,1,0:T(8,128)(2,1)}, ...) | async-done | bytes 3268624 | tf_op jit(solution)/shard_map/psum | solution.py:324
  461.0 4.3 convolution_convert_fusion.1
  465.3 1.8 copy.162
  467.2 4.0 all-to-all-start.1
  474.3 5.5 all-to-all-done.1
  479.8 3.4 all-to-all-start.2
  483.2 1.9 maximum_bitcast_fusion
  485.1 1.6 copy.168
  486.7 4.0 all-to-all-done.2
  490.6 4.5 all-to-all-start.3
  495.2 36.1 %all_gather.44 = bf16[512,896]{1,0:T(8,128)(2,1)S(1)} all-gather(bf16[128,896]{1,0:T(8,128)(2,1)S(1)} %copy-done.17), channel_id=1, replica_groups=mesh['dp'=4,'z'=4,'y'=4,'core'=2] {'dp'}, dimensions={0}, use_global_device_ids=true | all-gather | bytes 1146880 | tf_op jit(solution)/shard_map/all_gather | solution.py:368
  532.5 2.8 convolution_convert_fusion
  535.3 3.2 copy.169
  538.7 4.1 convert_element_type.189
  544.5 69.0 %psum.42 = f32[2944]{0:T(1024)S(1)} all-reduce(f32[2944]{0:T(1024)S(1)} %pad_maximum_fusion.8), channel_id=1, replica_groups=mesh['dp'=4,'z'=4,'y'=4,'core'=2] {'dp','z','y','core'}, use_global_device_ids=true, to_apply=%region_11.12 | all-reduce | flops 2944 | bytes 23552 | tf_op jit(solution)/shard_map/psum | solution.py:378
  615.4 2.2 fusion.20
  617.6 36.3 %all-reduce.10.cloned.1.call-done = (bf16[224,1152]{1,0:T(8,128)(2,1)}, bf16[224,896]{1,0:T(8,128)(2,1)}) async-done(((bf16[224,1152]{1,0:T(8,128)(2,1)}, bf16[224,896]{1,0:T(8,128)(2,1)}), (bf16[224,1152]{1,0:T(8,128)(2,1)}, bf16[224,896]{1,0:T(8,128)(2,1)})) %all-reduce.10.cloned.1.call-update) | async-done | bytes 917520 | tf_op jit(solution)/shard_map/psum | solution.py:377
  653.9 2.1 convert_element_type.179
  656.0 1.9 convert_element_type.183
  657.9 15.2 %all-gather.25.cloned.1.call-done = bf16[4,4,224,608]{3,2,0,1:T(8,128)(2,1)} async-done(((bf16[4,2,224,608]{3,2,0,1:T(8,128)(2,1)}), bf16[4,4,224,608]{3,2,0,1:T(8,128)(2,1)}) %all-gather.25.cloned.1.call-update) | async-done | bytes 4358160 | tf_op jit(solution)/shard_map/all_gather | solution.py:388
  673.1 3.2 convert_bitcast_fusion
  676.3 2.7 fusion.40
  679.0 5.7 copy.170
  684.7 7.8 %squeeze.27 = f32[224,4864]{1,0:T(8,128)} reshape(f32[1,224,4,2,608]{4,3,2,1,0:T(2,128)} %copy.170) | data formatting | bytes 8716288 | tf_op jit(solution)/shard_map/squeeze | solution.py:400
  692.5 8.0 %copy.171 = f32[1,224,4,2,608]{4,3,2,1,0:T(2,128)} copy(f32[1,224,4,2,608]{4,1,2,0,3:T(8,128)} %get-tuple-element.30) | data formatting | bytes 8716288 | tf_op jit(solution)/shard_map/slice | solution.py:401
  700.5 7.8 %squeeze.28 = f32[224,4864]{1,0:T(8,128)} reshape(f32[1,224,4,2,608]{4,3,2,1,0:T(2,128)} %copy.171) | data formatting | bytes 8716288 | tf_op jit(solution)/shard_map/squeeze | solution.py:401
  (195 shorter events, 47.6 us)
Async XLA Ops:
  7.2 192.2 %copy-start = (bf16[1216,896]{1,0:T(8,128)(2,1)S(1)}, bf16[1216,896]{1,0:T(8,128)(2,1)}, u32[]{:S(2)}) copy-start(bf16[1216,896]{1,0:T(8,128)(2,1)} %param.23) | copy-start | bytes 6537220
  7.2 36.3 %all-gather.11.cloned.1.call-start = ((), (), s32[]{:S(2)}) async-start(), calls=%async_computation.7 | async-start | bytes 2580480 | tf_op jit(solution)/shard_map/all_gather | solution.py:259
  7.9 83.2 %all-gather.13.cloned.1.call-start = ((), (), s32[]{:S(2)}) async-start(), calls=%async_computation.8 | async-start | bytes 2162688 | tf_op jit(solution)/shard_map/all_gather | solution.py:290
  21.5 0.6 copy-start.26
  21.5 24.2 %copy-start.24 = (f32[128,64]{0,1:T(8,128)}, f32[128,64]{0,1:T(8,128)S(1)}, u32[]{:S(2)}) copy-start(f32[128,64]{0,1:T(8,128)S(1)} %get-tuple-element.60) | copy-start | bytes 98308
  23.3 22.3 %copy-start.35 = (f32[128]{0:T(128)}, f32[128]{0:T(128)S(1)}, u32[]{:S(2)}) copy-start(f32[128]{0:T(128)S(1)} %fusion.21) | copy-start | bytes 1540
  23.3 22.4 %copy-start.31 = (f32[128]{0:T(128)}, f32[128]{0:T(128)S(1)}, u32[]{:S(2)}) copy-start(f32[128]{0:T(128)S(1)} %fusion.35) | copy-start | bytes 1540
  24.4 21.5 %copy-start.15 = (bf16[128,896]{1,0:T(8,128)(2,1)}, bf16[128,896]{1,0:T(8,128)(2,1)S(1)}, u32[]{:S(2)}) copy-start(bf16[128,896]{1,0:T(8,128)(2,1)S(1)} %fusion.14) | copy-start | bytes 688132
  24.4 23.1 %copy-start.6 = (s32[64]{0:T(128)S(1)}, s32[64]{0:T(128)}, u32[]{:S(2)}) copy-start(s32[64]{0:T(128)} %order_ref.3) | copy-start | bytes 772
  46.6 71.9 %all-gather.15.cloned.1.call-start = ((), (), s32[]{:S(2)}) async-start(), calls=%async_computation.9 | async-start | bytes 2007040 | tf_op jit(solution)/shard_map/all_gather | solution.py:264
  47.3 144.2 %all-gather.17.cloned.1.call-start = ((), (), s32[]{:S(2)}) async-start(), calls=%async_computation.10 | async-start | bytes 2064384 | tf_op jit(solution)/shard_map/all_gather | solution.py:302
  51.2 3.1 copy-start.13
  91.2 1.6 copy-start.5
  109.4 9.1 %copy-start.12 = (bf16[128,896]{1,0:T(8,128)(2,1)S(1)}, bf16[128,896]{1,0:T(8,128)(2,1)}, u32[]{:S(2)}) copy-start(bf16[128,896]{1,0:T(8,128)(2,1)} %param.12) | copy-start | bytes 688132
  120.6 123.1 %copy-start.7 = (f32[128,896]{1,0:T(8,128)}, f32[128,896]{1,0:T(8,128)S(1)}, u32[]{:S(2)}) copy-start(f32[128,896]{1,0:T(8,128)S(1)} %get-tuple-element.66) | copy-start | bytes 1376260
  120.6 123.1 %copy-start.29 = (f32[128]{0:T(128)}, f32[128]{0:T(128)S(1)}, u32[]{:S(2)}) copy-start(f32[128]{0:T(128)S(1)} %fusion.36) | copy-start | bytes 1540
  121.4 77.9 %all-gather.19.cloned.1.call-start = ((), (), s32[]{:S(2)}) async-start(), calls=%async_computation.12 | async-start | bytes 2064384 | tf_op jit(solution)/shard_map/all_gather | solution.py:274
  148.5 39.8 %all-to-all-start = ((bf16[4,2,224,608]{3,2,1,0:T(8,128)(2,1)}), bf16[4,2,224,608]{3,2,1,0:T(8,128)(2,1)}, u32[]{:S(2)}, u32[]{:S(2)}) async-start(bf16[4,2,224,608]{3,2,1,0:T(8,128)(2,1)} %bitcast.134), calls=%async_computation | async-start | bytes 4587520 | tf_op jit(solution)/shard_map/all_to_all | solution.py:270
  153.0 88.9 %reduce-scatter.6.cloned.1.call-start = ((), (), s32[]{:S(2)}) async-start(), calls=%async_computation.13 | async-start | bytes 2064384 | tf_op jit(solution)/shard_map/reduce_scatter | solution.py:315
  191.5 4.9 copy-start.21
  191.5 4.9 copy-start.37
  199.3 6.5 copy-start.23
  205.9 1.8 copy-start.39
  205.9 1.8 copy-start.38
  205.9 2.1 copy-start.22
  211.1 147.4 %reduce-scatter.8.cloned.1.call-start = ((), (), s32[]{:S(2)}) async-start(), calls=%async_computation.14 | async-start | bytes 2162688 | tf_op jit(solution)/shard_map/reduce_scatter | solution.py:342
  241.9 3.1 copy-start.11
  243.7 3.7 copy-start.33
  244.9 2.5 copy-start.16
  250.0 3.2 copy-start.19
  258.3 1.0 copy-start.2
  259.3 1.0 copy-start.3
  260.3 1.0 copy-start.4
  277.8 1.3 copy-start.1
  279.1 181.8 %all-reduce.12.cloned.1.call-start = ((), (), s32[]{:S(2)}) async-start(), calls=%async_computation.19 | async-start | bytes 6766592 | tf_op jit(solution)/shard_map/psum | solution.py:324
  296.9 235.6 %all-gather.21.cloned.1.call-start = ((), (), s32[]{:S(2)}) async-start(), calls=%async_computation.15 | async-start | bytes 1474560 | tf_op jit(solution)/shard_map/all_gather | solution.py:370
  300.2 2.6 copy-start.25
  301.5 2.5 copy-start.27
  302.8 1.2 copy-start.20
  361.2 177.4 %all-gather.23.cloned.1.call-start = ((), (), s32[]{:S(2)}) async-start(), calls=%async_computation.16 | async-start | bytes 3268608 | tf_op jit(solution)/shard_map/all_gather | solution.py:390
  461.0 154.4 %reduce-scatter.4.cloned.1.call-start = ((), (), s32[]{:S(2)}) async-start(), calls=%async_computation.11 | async-start | bytes 2064384 | tf_op jit(solution)/shard_map/reduce_scatter | solution.py:320
  465.3 5.9 copy-start.9
  467.2 12.6 %all-to-all-start.1 = ((bf16[4,128,224]{1,2,0:T(8,128)(2,1)}), bf16[4,128,224]{1,2,0:T(8,128)(2,1)}, u32[]{:S(2)}, u32[]{:S(2)}) async-start(bf16[4,128,224]{1,2,0:T(8,128)(2,1)} %bitcast.149), calls=%async_computation.4 | async-start | bytes 458752 | tf_op jit(solution)/shard_map/all_to_all | solution.py:363
  479.8 10.9 %all-to-all-start.2 = ((bf16[4,128,224]{1,2,0:T(8,128)(2,1)}), bf16[4,128,224]{1,2,0:T(8,128)(2,1)S(1)}, u32[]{:S(2)}, u32[]{:S(2)}) async-start(bf16[4,128,224]{1,2,0:T(8,128)(2,1)} %bitcast.38), calls=%async_computation.5 | async-start | bytes 458752 | tf_op jit(solution)/shard_map/all_to_all | solution.py:363
  486.7 8.5 %copy-start.17 = (bf16[128,896]{1,0:T(8,128)(2,1)S(1)}, bf16[128,896]{1,0:T(8,128)(2,1)}, u32[]{:S(2)}) copy-start(bf16[128,896]{1,0:T(8,128)(2,1)} %copy-done.16) | copy-start | bytes 688132
  490.6 44.7 %all-to-all-start.3 = ((bf16[4,2,224,608]{3,2,1,0:T(8,128)(2,1)}), bf16[4,2,224,608]{3,2,1,0:T(8,128)(2,1)}, u32[]{:S(2)}, u32[]{:S(2)}) async-start(bf16[4,2,224,608]{3,2,1,0:T(8,128)(2,1)} %copy.168), calls=%async_computation.6 | async-start | bytes 4587520 | tf_op jit(solution)/shard_map/all_to_all | solution.py:387
  495.2 158.8 %all-reduce.10.cloned.1.call-start = ((), (), s32[]{:S(2)}) async-start(), calls=%async_computation.18 | async-start | bytes 1835008 | tf_op jit(solution)/shard_map/psum | solution.py:377
  535.3 137.8 %all-gather.25.cloned.1.call-start = ((), (), s32[]{:S(2)}) async-start(), calls=%async_computation.17 | async-start | bytes 6881280 | tf_op jit(solution)/shard_map/all_gather | solution.py:388
  538.6 4.2 copy-start.14
  538.6 4.2 copy-start.32
  538.7 4.2 copy-start.10
  542.8 1.6 copy-start.28
  542.8 72.5 %copy-start.36 = (f32[128]{0:T(128)S(1)}, f32[128]{0:T(128)}, u32[]{:S(2)}) copy-start(f32[128]{0:T(128)} %copy-done.35) | copy-start | bytes 1540
  542.8 72.5 %copy-start.8 = (f32[128,896]{1,0:T(8,128)S(1)}, f32[128,896]{1,0:T(8,128)}, u32[]{:S(2)}) copy-start(f32[128,896]{1,0:T(8,128)} %copy-done.7) | copy-start | bytes 1376260
  542.9 72.5 %copy-start.18 = (bf16[128,896]{1,0:T(8,128)(2,1)S(1)}, bf16[128,896]{1,0:T(8,128)(2,1)}, u32[]{:S(2)}) copy-start(bf16[128,896]{1,0:T(8,128)(2,1)} %param.13) | copy-start | bytes 688132
  542.9 72.5 %copy-start.30 = (f32[128]{0:T(128)S(1)}, f32[128]{0:T(128)}, u32[]{:S(2)}) copy-start(f32[128]{0:T(128)} %copy-done.29) | copy-start | bytes 1540
  542.9 72.5 %copy-start.34 = (f32[128]{0:T(128)S(1)}, f32[128]{0:T(128)}, u32[]{:S(2)}) copy-start(f32[128]{0:T(128)} %copy-done.33) | copy-start | bytes 1540
Sparse Core Ops, SparseCore 0:
  9.7 33.7 all-gather.10
  46.7 44.4 all-gather.12
  92.8 25.5 all-gather.14
  121.6 25.0 all-gather.16
  148.2 29.9 all-gather.18
  211.2 30.6 reduce-scatter.5
  279.2 79.1 reduce-scatter.7
  362.8 98.0 all-reduce.11
  462.6 29.5 all-gather.20
  493.7 13.6 all-gather.22
  510.4 36.0 reduce-scatter.3
  550.2 103.6 all-reduce.9
  656.2 16.8 all-gather.24
